TPU v7x, 128 devices: a whole 4x4x4 slice. The times are simulated.
128 devices in a mesh: blk: 16 (over y_lo, z, core), row: 8 (over y_hi, x).
Axes of the slice: x: 4, y: 4 (y_hi: 2, y_lo: 2; y = y_hi * 2 + y_lo), z: 4, core: 2. Of those that a mesh axis runs over, the one named last changes fastest.
Arguments:
- image_embed: float32 [32768, 768], P(('blk', 'row')), may hold values from -16 to 16, as said below
- text_embed: float32 [32768, 768], P(('blk', 'row')), may hold values from -4 to 4
- logit_scale: float32 [1], replicated, may hold values from 7 to 14
Outputs:
- loss: float32 [1], replicated
- scale_grad: float32 [1], replicated
- image_grad: float32 [32768, 768], P(('blk', 'row'))
- text_grad: float32 [32768, 768], P(('blk', 'row'))
Inputs may be any that keep to these rules, and one draw needn't show every extreme that they name: Row i of image_embed and row i of text_embed describe the same pair.
All inputs are finite; a program needn't handle non-finite values.
Results may differ from a plain program's by a relative error of at most 0.0003.
Values sent between devices are 32-bit elements; how exact they have to be, the bound alone decides.
A program may use at most 128 MiB of HBM per device.

v0:
```python
import jax
import jax.numpy as jnp
from jax import lax
from jax.sharding import PartitionSpec as P

WINDOW = 4


def from_behind(block, axis, distance):
    devices = range(lax.axis_size(axis))
    route = [((i - distance) % len(devices), i) for i in devices]
    return lax.ppermute(block, axis, route)


def combine_parts(left_part, right_part):
    upper = jnp.maximum(left_part[0], right_part[0])
    joined = left_part[1] * jnp.exp(left_part[0] - upper) + right_part[1] * jnp.exp(
        right_part[0] - upper
    )
    return (upper, joined)


def shards(image_embed, text_embed, logit_scale):
    scale_value = logit_scale[0]
    my_rows = image_embed.shape[0]
    group_imgs = lax.all_gather(image_embed, "row", axis=0, tiled=True)

    def raw_scores(text_block):
        return lax.dot_general(
            group_imgs,
            text_block,
            (((1,), (1,)), ((), ())),
            precision=lax.Precision.HIGHEST,
            preferred_element_type=jnp.float32,
        )

    text_block = text_embed
    saved_blocks = []
    saved_raw = []
    for position in range(WINDOW):
        if position > 0:
            text_block, col_top, col_total = from_behind(
                (text_block, col_top, col_total), "blk", -1
            )
        raw_dot = raw_scores(text_block)
        scores = scale_value * raw_dot
        here_col_top = jnp.max(scores, axis=0)
        here_col_total = jnp.sum(jnp.exp(scores - here_col_top[None, :]), axis=0)
        here_row_top = jnp.max(scores, axis=1)
        here_row_total = jnp.sum(jnp.exp(scores - here_row_top[:, None]), axis=1)
        if position == 0:
            col_top, col_total = (here_col_top, here_col_total)
            row_top, row_total = (here_row_top, here_row_total)
        else:
            col_top, col_total = combine_parts((col_top, col_total), (here_col_top, here_col_total))
            row_top, row_total = combine_parts((row_top, row_total), (here_row_top, here_row_total))
        saved_blocks.append(text_block)
        saved_raw.append(raw_dot)
    group_top = lax.pmax(row_top, "row")
    group_total = lax.psum(row_total * jnp.exp(row_top - group_top), "row")
    image_lse = group_top + jnp.log(group_total)
    text_lse = col_top + jnp.log(col_total)
    image_part = jnp.zeros(group_imgs.shape, jnp.float32)
    text_part = jnp.zeros(text_embed.shape, jnp.float32)
    scale_sum = jnp.zeros((), jnp.float32)
    for back_step in range(WINDOW):
        if back_step > 0:
            text_block, text_lse, text_part = from_behind(
                (text_block, text_lse, text_part), "blk", 1
            )
        raw_dot = raw_scores(text_block)
        scores = scale_value * raw_dot
        weight = 0.5 * jnp.exp(scores - image_lse[:, None]) + 0.5 * jnp.exp(
            scores - text_lse[None, :]
        )
        image_part = image_part + scale_value * jnp.dot(
            weight, text_block, precision=lax.Precision.HIGHEST, preferred_element_type=jnp.float32
        )
        text_part = text_part + scale_value * lax.dot_general(
            weight,
            group_imgs,
            (((0,), (0,)), ((), ())),
            precision=lax.Precision.HIGHEST,
            preferred_element_type=jnp.float32,
        )
        scale_sum = scale_sum + jnp.sum(weight * raw_dot)
    row_start = lax.axis_index("row") * my_rows
    my_lse = lax.dynamic_slice_in_dim(image_lse, row_start, my_rows)
    image_grad = (
        lax.psum_scatter(image_part, "row", scatter_dimension=0, tiled=True)
        - scale_value * text_embed
    )
    text_grad = text_part - scale_value * image_embed
    positive = jnp.sum(image_embed * text_embed, axis=1)
    loss_term = 0.5 * jnp.sum(my_lse) + 0.5 * jnp.sum(text_lse) - scale_value * jnp.sum(positive)
    scale_term = scale_sum - jnp.sum(positive)
    loss_sum, scale_total = lax.psum((loss_term, scale_term), ("blk", "row"))
    pair_count = my_rows * lax.axis_size("blk") * lax.axis_size("row")
    return (
        (loss_sum / pair_count).reshape(1),
        (scale_total / pair_count).reshape(1),
        image_grad,
        text_grad,
    )


def solution(mesh):
    in_specs = (P(("blk", "row"), None), P(("blk", "row"), None), P())
    out_specs = (P(), P(), P(("blk", "row"), None), P(("blk", "row"), None))
    return jax.shard_map(shards, mesh=mesh, in_specs=in_specs, out_specs=out_specs, check_vma=False)
```

profile of v0, /device:TPU:9, one launch (start us, length us, event | category | flops | bytes accessed | tf_op | source)
XLA Modules:
  0.0 447.5 jit_solution(349448317702317288)
XLA Ops:
  8.7 11.4 %collective-permute-done = f32[256,768]{1,0:T(8,128)S(1)} collective-permute-done((f32[256,768]{1,0:T(8,128)}, f32[256,768]{1,0:T(8,128)S(1)}, u32[]{:S(2)}, u32[]{:S(2)}) %collective-permute-start) | collective-permute-done | bytes 786464 | tf_op jit(solution)/shard_map/ppermute | solution.py:12
  21.9 10.0 %collective-permute-done.1 = f32[256,768]{1,0:T(8,128)S(1)} collective-permute-done((f32[256,768]{1,0:T(8,128)S(1)}, f32[256,768]{1,0:T(8,128)S(1)}, u32[]{:S(2)}, u32[]{:S(2)}) %collective-permute-start.1) | collective-permute-done | bytes 786464 | tf_op jit(solution)/shard_map/ppermute | solution.py:12
  31.9 9.6 %collective-permute-start.2 = (f32[256,768]{1,0:T(8,128)S(1)}, f32[256,768]{1,0:T(8,128)}, u32[]{:S(2)}, u32[]{:S(2)}) collective-permute-start(f32[256,768]{1,0:T(8,128)S(1)} %collective-permute-done.1), channel_id=1, source_target_pairs={{8,0},{16,8},{24,16},{32,24},{40,32},{48,40},{56,48},{64,56},{72,6... | collective-permute-start | bytes 2359304 | tf_op jit(solution)/shard_map/ppermute | solution.py:12
  43.7 20.7 %collective-permute-done.12 = f32[256,768]{1,0:T(8,128)S(1)} collective-permute-done((f32[256,768]{1,0:T(8,128)}, f32[256,768]{1,0:T(8,128)S(1)}, u32[]{:S(2)}, u32[]{:S(2)}) %collective-permute-start.12) | collective-permute-done | bytes 786464 | tf_op jit(solution)/shard_map/ppermute | solution.py:12
  65.1 30.3 %collective-permute-done.13 = f32[256,768]{1,0:T(8,128)S(1)} collective-permute-done((f32[256,768]{1,0:T(8,128)S(1)}, f32[256,768]{1,0:T(8,128)S(1)}, u32[]{:S(2)}, u32[]{:S(2)}) %collective-permute-start.13) | collective-permute-done | bytes 786464 | tf_op jit(solution)/shard_map/ppermute | solution.py:12
  95.4 10.1 %all-gather.2.cloned.1.call-done = f32[2048,768]{1,0:T(8,128)} async-done(((f32[256,768]{1,0:T(8,128)}), f32[2048,768]{1,0:T(8,128)}) %all-gather.2.cloned.1.call-update) | async-done | bytes 6291472 | tf_op jit(solution)/shard_map/all_gather | solution.py:26
  105.5 7.9 %fusion.58 = (f32[256]{0:T(256)S(1)}, f32[2048]{0:T(1024)S(1)}, f32[2048,256]{1,0:T(8,128)S(1)}) fusion(f32[2048,768]{1,0:T(8,128)} %all-gather.2.cloned.1.call-done, f32[256,768]{1,0:T(8,128)} %param.4, f32[]{:T(128)} %bitcast.25), kind=kOutput, calls=%fused_computation.89 | convolution fusion | flops 4833409024 | bytes 9184260 | tf_op jit(solution)/shard_map/dot_general | solution.py:29
  116.1 7.0 %collective-permute-start.6 = (f32[256]{0:T(256)S(1)}, f32[256]{0:T(256)S(1)}, u32[]{:S(2)}, u32[]{:S(2)}) collective-permute-start(f32[256]{0:T(256)S(1)} %get-tuple-element.4), channel_id=1, source_target_pairs={{8,0},{16,8},{24,16},{32,24},{40,32},{48,40},{56,48},{64,56},{72,6... | collective-permute-start | bytes 3080 | tf_op jit(solution)/shard_map/ppermute | solution.py:12
  123.1 6.7 %fusion.57 = (f32[256]{0:T(256)S(1)}, f32[2048]{0:T(1024)S(1)}, f32[2048,256]{1,0:T(8,128)}) fusion(f32[2048,768]{1,0:T(8,128)S(1)} %copy-done, f32[256,768]{1,0:T(8,128)S(1)} %collective-permute-done, f32[]{:T(128)} %bitcast.36), kind=kOutput, calls=%fused_computation.88 | convolution fusion | flops 4833409024 | bytes 9184260 | tf_op jit(solution)/shard_map/dot_general | solution.py:29
  129.8 6.6 %fusion.56 = (f32[256]{0:T(256)S(1)}, f32[2048]{0:T(1024)S(1)}, f32[2048,256]{1,0:T(8,128)}) fusion(f32[2048,768]{1,0:T(8,128)S(1)} %copy-done, f32[256,768]{1,0:T(8,128)S(1)} %collective-permute-done.1, f32[]{:T(128)} %bitcast.39), kind=kOutput, calls=%fused_computation.87 | convolution fusion | flops 4833409024 | bytes 9184260 | tf_op jit(solution)/shard_map/dot_general | solution.py:29
  136.4 6.5 %multiply_reduce_fusion.4 = (f32[256]{0:T(256)S(1)}, f32[2048]{0:T(1024)S(1)}, f32[2048,256]{1,0:T(8,128)S(1)}) fusion(f32[]{:T(128)} %bitcast.37, f32[2048,768]{1,0:T(8,128)S(1)} %copy-done, f32[256,768]{1,0:T(8,128)} %collective-permute-done.2), kind=kOutput, calls=%fused_computation.20 | convolution fusion | flops 4833409024 | bytes 9184260 | tf_op jit(solution)/shard_map/dot_general | solution.py:29
  142.9 16.8 %pmax.7 = f32[2048]{0:T(1024)S(1)} all-reduce(f32[2048]{0:T(1024)S(1)} %get-tuple-element.30), channel_id=1, replica_groups=mesh['blk'=16,'row'=8] {'row'}, use_global_device_ids=true, to_apply=%region_4.0 | all-reduce | flops 2048 | bytes 16384 | tf_op jit(solution)/shard_map/pmax | solution.py:59
  164.3 8.7 %fusion.60 = f32[2048,256]{1,0:T(8,128)} fusion(f32[2048,768]{1,0:T(8,128)} %all-gather.2.cloned.1.call-done, f32[256,768]{1,0:T(8,128)S(1)} %copy-done.11), kind=kOutput, calls=%fused_computation.91 | convolution fusion | flops 4831838208 | bytes 9175040 | tf_op jit(solution)/shard_map/dot_general | solution.py:29
  173.0 6.6 %fusion.61 = f32[2048,256]{1,0:T(8,128)} fusion(f32[2048,768]{1,0:T(8,128)S(1)} %bitcast.42, f32[256,768]{1,0:T(8,128)S(1)} %collective-permute-done.13), kind=kOutput, calls=%fused_computation.92 | convolution fusion | flops 4831838208 | bytes 9175040 | tf_op jit(solution)/shard_map/dot_general | solution.py:29
  183.8 17.1 %psum.21 = f32[2048]{0:T(1024)S(1)} all-reduce(f32[2048]{0:T(1024)S(1)} %exponential_multiply_fusion), channel_id=1, replica_groups=mesh['blk'=16,'row'=8] {'row'}, use_global_device_ids=true, to_apply=%region_9.0 | all-reduce | flops 2048 | bytes 16384 | tf_op jit(solution)/shard_map/psum | solution.py:60
  208.2 6.9 %fusion.1 = f32[2048,768]{1,0:T(8,128)S(1)} fusion(f32[256,768]{1,0:T(8,128)} %collective-permute-done.2, f32[2048,256]{1,0:T(8,128)S(1)} %get-tuple-element.35, f32[256]{0:T(256)S(1)} %log_add_fusion.1, f32[2048]{0:T(1024)S(1)} %log_add_fusion, f32[]{:T(128)} %bitcast.34), kind=kOutput, calls=%fused_computation.23 | convolution fusion | flops 4834459648 | bytes 9184260 | tf_op jit(solution)/shard_map/dot_general | solution.py:76
  231.9 10.3 %multiply_reduce_fusion = (f32[]{:T(128)}, f32[]{:T(128)}, f32[]{:T(128)}, f32[]{:T(128)}, f32[2048,256]{1,0:T(8,128)S(1)}) fusion(f32[256]{0:T(256)S(1)} %collective-permute-done.11, f32[2048]{0:T(1024)S(1)} %log_add_fusion, f32[]{:T(128)} %bitcast.40, f32[2048,256]{1,0:T(8,128)S(1)} %copy-done.4, f32[256]{0:T(256)S(1)} %collective-permute-done.9, ...), kind=kOutput, calls=%fused_computation.4 | convolution fusion | flops 4846518272 | bytes 15478804 | tf_op jit(solution)/shard_map/dot_general | solution.py:29
  243.5 9.3 %add_multiply_fusion = f32[2048,768]{1,0:T(8,128)} fusion(f32[2048,768]{1,0:T(8,128)S(1)} %fusion.5, f32[2048,768]{1,0:T(8,128)S(1)} %fusion.1, f32[2048,768]{1,0:T(8,128)S(1)} %fusion.3, f32[256,768]{1,0:T(8,128)} %collective-permute-done.14, f32[]{:T(128)} %bitcast.27, f32[2048,256]{1,0:T(8,128)S(1)} %get-tuple-element.39, ...), kind=kOutput, calls=%fused_computation | convolution fusion | flops 4840751104 | bytes 28058628 | tf_op jit(solution)/shard_map/dot_general | solution.py:76
  252.9 14.6 %fusion.10 = f32[256,768]{1,0:T(8,128)S(1)} fusion(f32[2048,768]{1,0:T(8,128)} %all-gather.2.cloned.1.call-done, f32[2048,256]{1,0:T(8,128)} %copy-done.1, f32[256]{0:T(256)S(1)} %log_add_fusion.1, f32[2048]{0:T(1024)S(1)} %log_add_fusion, f32[]{:T(128)} %bitcast.35), kind=kOutput, calls=%fused_computation.32 | convolution fusion | flops 4834656256 | bytes 9184260 | tf_op jit(solution)/shard_map/dot_general | solution.py:79
  279.3 8.9 %collective-permute-done.16 = f32[256,768]{1,0:T(8,128)S(1)} collective-permute-done((f32[256,768]{1,0:T(8,128)S(1)}, f32[256,768]{1,0:T(8,128)S(1)}, u32[]{:S(2)}, u32[]{:S(2)}) %collective-permute-start.16) | collective-permute-done | bytes 786464 | tf_op jit(solution)/shard_map/ppermute | solution.py:12
  288.2 7.0 %fusion.11 = f32[256,768]{1,0:T(8,128)} fusion(f32[256,768]{1,0:T(8,128)S(1)} %collective-permute-done.16, f32[2048,768]{1,0:T(8,128)S(1)} %bitcast.46, f32[2048,256]{1,0:T(8,128)S(1)} %copy-done.3, f32[256]{0:T(256)S(1)} %collective-permute-done.10, f32[2048]{0:T(1024)S(1)} %log_add_fusion, f32[]{:T(128)} %bitcast.31), kind=kOutput, calls=%fused_computation.33 | convolution fusion | flops 4834852864 | bytes 9970692 | tf_op jit(solution)/shard_map/dot_general | solution.py:79
  302.8 56.0 %reduce-scatter.2.cloned.1.call-done = f32[256,768]{1,0:T(8,128)} async-done(((f32[2048,768]{1,0:T(8,128)}), f32[256,768]{1,0:T(8,128)}) %reduce-scatter.2.cloned.1.call-update) | async-done | bytes 786448 | tf_op jit(solution)/shard_map/reduce_scatter | solution.py:90
  363.0 9.5 %fusion.13 = f32[256,768]{1,0:T(8,128)} fusion(f32[256,768]{1,0:T(8,128)} %collective-permute-done.17, f32[2048,768]{1,0:T(8,128)} %all-gather.2.cloned.1.call-done, f32[2048,256]{1,0:T(8,128)S(1)} %copy-done.8, f32[256]{0:T(256)S(1)} %collective-permute-done.11, f32[2048]{0:T(1024)S(1)} %log_add_fusion, f32[]{:T(128)} %bitcast.29, f32[256,768]{1,0:T(8,128)S(1)} %copy-done.9), kind=kOutput, calls=%fused_computation.35 | convolution fusion | flops 4835246080 | bytes 10757124 | tf_op jit(solution)/shard_map/dot_general | solution.py:79
  372.5 64.4 %all-reduce = (f32[]{:T(128)}, f32[]{:T(128)}) all-reduce(f32[]{:T(128)S(6)} %sub.202, f32[]{:T(128)S(6)} %sub.216), channel_id=1, replica_groups=mesh['blk'=16,'row'=8] {'blk','row'}, use_global_device_ids=true, to_apply=%region_21.0 | all-reduce | flops 2 | bytes 16 | tf_op jit(solution)/shard_map/psum | solution.py:97
  (91 shorter events, 60.8 us)
Async XLA Ops:
  7.2 98.4 %all-gather.2.cloned.1.call-start = ((), (), s32[]{:S(2)}) async-start(), calls=%async_computation.1 | async-start | bytes 7077888 | tf_op jit(solution)/shard_map/all_gather | solution.py:26
  7.9 350.8 %reduce-scatter.2.cloned.1.call-start = ((), (), s32[]{:S(2)}) async-start(), calls=%async_computation.2 | async-start | bytes 7077888 | tf_op jit(solution)/shard_map/reduce_scatter | solution.py:90
  7.9 12.2 %collective-permute-start = (f32[256,768]{1,0:T(8,128)}, f32[256,768]{1,0:T(8,128)S(1)}, u32[]{:S(2)}, u32[]{:S(2)}) collective-permute-start(f32[256,768]{1,0:T(8,128)} %param.4), channel_id=1, source_target_pairs={{8,0},{16,8},{24,16},{32,24},{40,32},{48,40},{56,48},{64,56},{72,6... | collective-permute-start | bytes 2359304 | tf_op jit(solution)/shard_map/ppermute | solution.py:12
  20.1 11.8 %collective-permute-start.1 = (f32[256,768]{1,0:T(8,128)S(1)}, f32[256,768]{1,0:T(8,128)S(1)}, u32[]{:S(2)}, u32[]{:S(2)}) collective-permute-start(f32[256,768]{1,0:T(8,128)S(1)} %collective-permute-done), channel_id=1, source_target_pairs={{8,0},{16,8},{24,16},{32,24},{40,32},{48,40},{56,48},{64,56},{72,6... | collective-permute-start | bytes 2359304 | tf_op jit(solution)/shard_map/ppermute | solution.py:12
  31.9 11.8 %collective-permute-start.2 = (f32[256,768]{1,0:T(8,128)S(1)}, f32[256,768]{1,0:T(8,128)}, u32[]{:S(2)}, u32[]{:S(2)}) collective-permute-start(f32[256,768]{1,0:T(8,128)S(1)} %collective-permute-done.1), channel_id=1, source_target_pairs={{8,0},{16,8},{24,16},{32,24},{40,32},{48,40},{56,48},{64,56},{72,6... | collective-permute-start | bytes 2359304 | tf_op jit(solution)/shard_map/ppermute | solution.py:12
  43.7 20.8 %collective-permute-start.12 = (f32[256,768]{1,0:T(8,128)}, f32[256,768]{1,0:T(8,128)S(1)}, u32[]{:S(2)}, u32[]{:S(2)}) collective-permute-start(f32[256,768]{1,0:T(8,128)} %collective-permute-done.2), channel_id=1, source_target_pairs={{120,0},{0,8},{8,16},{16,24},{24,32},{32,40},{40,48},{48,56},{56,6... | collective-permute-start | bytes 2359304 | tf_op jit(solution)/shard_map/ppermute | solution.py:12
  64.5 30.9 %copy-start.10 = (f32[256,768]{1,0:T(8,128)}, f32[256,768]{1,0:T(8,128)S(1)}, u32[]{:S(2)}) copy-start(f32[256,768]{1,0:T(8,128)S(1)} %collective-permute-done.12) | copy-start | bytes 2359300
  64.5 30.9 %collective-permute-start.13 = (f32[256,768]{1,0:T(8,128)S(1)}, f32[256,768]{1,0:T(8,128)S(1)}, u32[]{:S(2)}, u32[]{:S(2)}) collective-permute-start(f32[256,768]{1,0:T(8,128)S(1)} %collective-permute-done.12), channel_id=1, source_target_pairs={{120,0},{0,8},{8,16},{16,24},{24,32},{32,40},{40,48},{48,56},{56,6... | collective-permute-start | bytes 2359304 | tf_op jit(solution)/shard_map/ppermute | solution.py:12
  95.4 136.4 %collective-permute-start.14 = (f32[256,768]{1,0:T(8,128)S(1)}, f32[256,768]{1,0:T(8,128)}, u32[]{:S(2)}, u32[]{:S(2)}) collective-permute-start(f32[256,768]{1,0:T(8,128)S(1)} %collective-permute-done.13), channel_id=1, source_target_pairs={{120,0},{0,8},{8,16},{16,24},{24,32},{32,40},{40,48},{48,56},{56,6... | collective-permute-start | bytes 2359304 | tf_op jit(solution)/shard_map/ppermute | solution.py:12
  113.4 66.2 %collective-permute-start.3 = (f32[256]{0:T(256)S(1)}, f32[256]{0:T(256)S(1)}, u32[]{:S(2)}, u32[]{:S(2)}) collective-permute-start(f32[256]{0:T(256)S(1)} %get-tuple-element.14), channel_id=1, source_target_pairs={{8,0},{16,8},{24,16},{32,24},{40,32},{48,40},{56,48},{64,56},{72,6... | collective-permute-start | bytes 3080 | tf_op jit(solution)/shard_map/ppermute | solution.py:12
  116.1 63.5 %collective-permute-start.6 = (f32[256]{0:T(256)S(1)}, f32[256]{0:T(256)S(1)}, u32[]{:S(2)}, u32[]{:S(2)}) collective-permute-start(f32[256]{0:T(256)S(1)} %get-tuple-element.4), channel_id=1, source_target_pairs={{8,0},{16,8},{24,16},{32,24},{40,32},{48,40},{56,48},{64,56},{72,6... | collective-permute-start | bytes 3080 | tf_op jit(solution)/shard_map/ppermute | solution.py:12
  142.9 88.9 %copy-start.1 = (f32[2048,256]{1,0:T(8,128)}, f32[2048,256]{1,0:T(8,128)S(1)}, u32[]{:S(2)}) copy-start(f32[2048,256]{1,0:T(8,128)S(1)} %get-tuple-element.35) | copy-start | bytes 6291460
  179.6 21.3 %collective-permute-start.4 = (f32[256]{0:T(256)S(1)}, f32[256]{0:T(256)S(1)}, u32[]{:S(2)}, u32[]{:S(2)}) collective-permute-start(f32[256]{0:T(256)S(1)} %get-tuple-element.29), channel_id=1, source_target_pairs={{8,0},{16,8},{24,16},{32,24},{40,32},{48,40},{56,48},{64,56},{72,6... | collective-permute-start | bytes 3080 | tf_op jit(solution)/shard_map/ppermute | solution.py:12
  183.7 17.2 %collective-permute-start.7 = (f32[256]{0:T(256)S(1)}, f32[256]{0:T(256)S(1)}, u32[]{:S(2)}, u32[]{:S(2)}) collective-permute-start(f32[256]{0:T(256)S(1)} %get-tuple-element.28), channel_id=1, source_target_pairs={{8,0},{16,8},{24,16},{32,24},{40,32},{48,40},{56,48},{64,56},{72,6... | collective-permute-start | bytes 3080 | tf_op jit(solution)/shard_map/ppermute | solution.py:12
  201.0 7.0 %collective-permute-start.5 = (f32[256]{0:T(256)S(1)}, f32[256]{0:T(256)S(1)}, u32[]{:S(2)}, u32[]{:S(2)}) collective-permute-start(f32[256]{0:T(256)S(1)} %get-tuple-element.27), channel_id=1, source_target_pairs={{8,0},{16,8},{24,16},{32,24},{40,32},{48,40},{56,48},{64,56},{72,6... | collective-permute-start | bytes 3080 | tf_op jit(solution)/shard_map/ppermute | solution.py:12
  205.1 3.0 collective-permute-start.8
  208.1 7.0 %collective-permute-start.9 = (f32[256]{0:T(256)S(1)}, f32[256]{0:T(256)S(1)}, u32[]{:S(2)}, u32[]{:S(2)}) collective-permute-start(f32[256]{0:T(256)S(1)} %log_add_fusion.1), channel_id=1, source_target_pairs={{120,0},{0,8},{8,16},{16,24},{24,32},{32,40},{40,48},{48,56},{56,6... | collective-permute-start | bytes 3080 | tf_op jit(solution)/shard_map/ppermute | solution.py:12
  215.1 8.2 %collective-permute-start.10 = (f32[256]{0:T(256)S(1)}, f32[256]{0:T(256)S(1)}, u32[]{:S(2)}, u32[]{:S(2)}) collective-permute-start(f32[256]{0:T(256)S(1)} %collective-permute-done.9), channel_id=1, source_target_pairs={{120,0},{0,8},{8,16},{16,24},{24,32},{32,40},{40,48},{48,56},{56,6... | collective-permute-start | bytes 3080 | tf_op jit(solution)/shard_map/ppermute | solution.py:12
  223.3 8.5 %collective-permute-start.11 = (f32[256]{0:T(256)S(1)}, f32[256]{0:T(256)S(1)}, u32[]{:S(2)}, u32[]{:S(2)}) collective-permute-start(f32[256]{0:T(256)S(1)} %collective-permute-done.10), channel_id=1, source_target_pairs={{120,0},{0,8},{8,16},{16,24},{24,32},{32,40},{40,48},{48,56},{56,6... | collective-permute-start | bytes 3080 | tf_op jit(solution)/shard_map/ppermute | solution.py:12
  267.4 9.1 %collective-permute-start.15 = (f32[256,768]{1,0:T(8,128)S(1)}, f32[256,768]{1,0:T(8,128)S(1)}, u32[]{:S(2)}, u32[]{:S(2)}) collective-permute-start(f32[256,768]{1,0:T(8,128)S(1)} %fusion.10), channel_id=1, source_target_pairs={{120,0},{0,8},{8,16},{16,24},{24,32},{32,40},{40,48},{48,56},{56,6... | collective-permute-start | bytes 2359304 | tf_op jit(solution)/shard_map/ppermute | solution.py:12
  276.6 11.7 %collective-permute-start.16 = (f32[256,768]{1,0:T(8,128)S(1)}, f32[256,768]{1,0:T(8,128)S(1)}, u32[]{:S(2)}, u32[]{:S(2)}) collective-permute-start(f32[256,768]{1,0:T(8,128)S(1)} %add.102), channel_id=1, source_target_pairs={{120,0},{0,8},{8,16},{16,24},{24,32},{32,40},{40,48},{48,56},{56,6... | collective-permute-start | bytes 2359304 | tf_op jit(solution)/shard_map/ppermute | solution.py:12
  288.2 70.5 %copy-start.9 = (f32[256,768]{1,0:T(8,128)S(1)}, f32[256,768]{1,0:T(8,128)}, u32[]{:S(2)}) copy-start(f32[256,768]{1,0:T(8,128)} %param.3) | copy-start | bytes 2359300
  295.3 67.8 %copy-start.8 = (f32[2048,256]{1,0:T(8,128)S(1)}, f32[2048,256]{1,0:T(8,128)}, u32[]{:S(2)}) copy-start(f32[2048,256]{1,0:T(8,128)} %copy-done.7) | copy-start | bytes 6291460
  295.3 67.8 %collective-permute-start.17 = (f32[256,768]{1,0:T(8,128)}, f32[256,768]{1,0:T(8,128)}, u32[]{:S(2)}, u32[]{:S(2)}) collective-permute-start(f32[256,768]{1,0:T(8,128)} %fusion.11), channel_id=1, source_target_pairs={{120,0},{0,8},{8,16},{16,24},{24,32},{32,40},{40,48},{48,56},{56,6... | collective-permute-start | bytes 2359304 | tf_op jit(solution)/shard_map/ppermute | solution.py:12
  (15 other events, 148.9 us)
Sparse Core Ops, SparseCore 0:
  10.3 95.1 all-gather.1
  253.0 105.7 reduce-scatter.1
where the time goes:
time: 455 us; the launch traced here: 448 us
  waiting for transfers between devices  156 us (34%)
  matrix products  118 us (26%)
  blocking collectives  98.3 us (22%)
  starting transfers between devices  40.1 us (9%)
  between operations  23.9 us (5%)
  other arithmetic  9.85 us (2%)
    ppermute x18, waiting for transfers between devices, from_behind(): return lax.ppermute(block, axis, route)  89.4 us
    psum x1, blocking collectives, shards(): loss_sum, scale_total = lax.psum((loss_term, scale_term), ('blk', 'row'))  64.4 us
    reduce_scatter x1, waiting for transfers between devices, shards(): lax.psum_scatter(image_part, 'row', scatter_dimension=0, tiled=True)  56 us
    dot_general x7, matrix products, raw_scores(): lax.dot_general(group_imgs, text_block, (((1,), (1,)), ((), ())), precisi...  53.3 us
    ppermute x18, starting transfers between devices, from_behind(): return lax.ppermute(block, axis, route)  40 us
    dot_general x4, matrix products, shards(): lax.dot_general(weight, group_imgs, (((0,), (0,)), ((), ())), precision=l...  37.2 us
    dot_general x4, matrix products, shards(): jnp.dot(weight, text_block, precision=lax.Precision.HIGHEST, preferred_el...  27.4 us
    psum x1, blocking collectives, shards(): group_total = lax.psum(row_total * jnp.exp(row_top - group_top), 'row')  17.1 us
  transfers between devices with their start and end apart: 20, of which 11 were waited for; matrix products, arithmetic and copies ran while one was open for 22% of the time, Pallas kernels for 0%

commit v1 on v0

v1 whole, which is shorter than its diff:
```python
import functools

import jax
import jax.numpy as jnp
from jax import lax
from jax.experimental import pallas as pl
from jax.experimental.pallas import tpu as pltpu
from jax.sharding import PartitionSpec as P

MESH = pl.DeviceIdType.MESH
F32 = jnp.float32
BF16 = jnp.bfloat16
WINDOW = 4
N_IMG = 4
OFFSETS = (0, 1, 3, 2)
N_TXT = 8
LOW = -1e30

DELTAS = [(d, g) for d in (-3, -2, -1, 0, 1, 2, 3) for g in (0, 1) if (d, g) != (0, 0)]


class Place:
    def __init__(self, y_lo, z, core, y_hi, x):
        self.y_lo, self.z, self.core, self.y_hi, self.x = y_lo, z, core, y_hi, x

    def device(self):
        return (self.y_lo * 8 + self.z * 2 + self.core, self.y_hi * 4 + self.x)

    def move(self, x=0, h=0, c=0, z=0, yl=0, blk=0, plane=0):
        y_lo, zz, core = self.y_lo, self.z, self.core
        if blk:
            b = lax.rem(y_lo * 8 + zz * 2 + core + blk + 16, 16)
            y_lo, zz, core = b // 8, lax.rem(b // 2, 4), lax.rem(b, 2)
        if plane:
            k = lax.rem(y_lo * 4 + zz + plane + 8, 8)
            y_lo, zz = k // 4, lax.rem(k, 4)
        if z:
            zz = lax.rem(zz + z + 4, 4)
        if c:
            core = 1 - core
        if yl:
            y_lo = 1 - y_lo
        y_hi = 1 - self.y_hi if h else self.y_hi
        xx = lax.rem(self.x + x + 4, 4) if x else self.x
        return Place(y_lo, zz, core, y_hi, xx)


def here():
    b, r = lax.axis_index("blk"), lax.axis_index("row")
    return Place(b // 8, lax.rem(b // 2, 4), lax.rem(b, 2), r // 4, lax.rem(r, 4))


def split(value):
    high = value.astype(BF16)
    return high, (value - high.astype(F32)).astype(BF16)


def kernel(
    rows,
    scale_ref,
    img_ref,
    txt_ref,
    sums_ref,
    img_out,
    txt_out,
    img_in,
    txt_in,
    relay_in,
    img_hi,
    img_lo,
    txt_hi,
    txt_lo,
    scores,
    r_hi,
    r_lo,
    row_top,
    row_sum,
    row_stat,
    col_stat,
    row_got,
    col_got,
    img_part,
    txt_part,
    chip_got,
    ring_got,
    relay_got,
    relay_back,
    pair_got,
    img_got,
    img_half,
    sum_send,
    sum_got,
    send_sem,
    recv_sem,
):
    me = here()
    is0, is1 = me.core == 0, me.core == 1
    half = rows // 2
    top, bottom = pl.ds(0, half), pl.ds(half, half)
    scale = scale_ref[0]
    pending = []
    slots = {}

    def sem(name):
        return slots.setdefault(name, len(slots))

    def copy(name, src, dst, place):
        return pltpu.make_async_remote_copy(
            src_ref=src,
            dst_ref=dst,
            send_sem=send_sem.at[len(pending)],
            recv_sem=recv_sem.at[sem(name)],
            device_id=place.device(),
            device_id_type=MESH,
        )

    def send(name, src, dst, place, when=None):
        c = copy(name, src, dst, place)
        if when is None:
            c.start()
        else:
            pl.when(when)(c.start)
        pending.append((c, when))

    def arrive(name, dst, when=None):
        c = copy(name, dst, dst, me.move(h=1))
        if when is None:
            c.wait_recv()
        else:
            pl.when(when)(c.wait_recv)

    source_plane_from_relay = me.move(z=-1)
    relay_to = source_plane_from_relay.move(plane=-2)
    relay_to = Place(relay_to.y_lo, relay_to.z, 1 - me.core, me.y_hi, me.x)
    relay_from = me.move(plane=2).move(z=1)
    relay_from = Place(relay_from.y_lo, relay_from.z, 1 - me.core, me.y_hi, me.x)

    partners = [me.move(x=1), me.move(x=2), me.move(x=3), me.move(h=1), me.move(c=1)]
    partners += [me.move(z=1), me.move(z=2), me.move(z=3), me.move(yl=1)]
    partners += [relay_to, relay_to.move(h=1), relay_from, relay_from.move(h=1)]
    partners += [me.move(blk=d, h=g) for d, g in DELTAS if d != 0]
    barrier = pltpu.get_barrier_semaphore()
    for p in partners:
        pl.semaphore_signal(barrier, inc=1, device_id=p.device(), device_id_type=MESH)
    pl.semaphore_wait(barrier, len(partners))

    def tx(d, e):
        return txt_in.at[2 * d + e - 1]

    at0 = me.z == 0
    not0 = me.z != 0
    prev = [me.move(blk=-1), me.move(blk=-2)]
    send("i1", img_ref, img_in.at[0], me.move(x=-1))
    send("i2", img_ref, img_in.at[1], me.move(x=1))
    send("t01", txt_ref, tx(0, 1), me.move(h=1))
    send("t10", txt_ref, tx(1, 0), me.move(blk=-1))
    send("t20", txt_ref, tx(2, 0), me.move(blk=-2), is1)
    send("relay", txt_ref, relay_in, me.move(z=1), is0)
    send("t11", txt_ref, tx(1, 1), me.move(blk=-1, h=1), is0 & at0)
    send("t21", txt_ref, tx(2, 1), me.move(blk=-2, h=1), is1 & at0)

    def img_ready(i, value):
        high, low = split(value)
        at = pl.ds(i * rows, rows)
        img_hi[at, :] = high
        img_lo[at, :] = low

    def txt_ready(t, value):
        high, low = split(value)
        at = pl.ds(t * rows, rows)
        txt_hi[at, :] = high
        txt_lo[at, :] = low

    row_top[...] = jnp.full(row_top.shape, LOW, F32)
    row_sum[...] = jnp.zeros(row_sum.shape, F32)
    img_ready(0, img_ref[...])
    txt_ready(0, txt_ref[...])

    nt = (((1,), (1,)), ((), ()))
    tn = (((0,), (0,)), ((), ()))
    nn = (((1,), (0,)), ((), ()))

    def dot(a, b, dims):
        return lax.dot_general(a, b, dims, preferred_element_type=F32)

    def score_tiles(t, first, last):
        cols = pl.ds(t * rows, rows)

        def tile(i, carry):
            at = pl.ds(pl.multiple_of(i * rows, rows), rows)
            raw = dot(img_hi[at, :], txt_hi[cols, :], nt)
            raw += dot(img_hi[at, :], txt_lo[cols, :], nt)
            raw += dot(img_lo[at, :], txt_hi[cols, :], nt)
            scores[at, cols] = scale * raw
            return carry

        lax.fori_loop(first, last, tile, 0)

    def block_stats(t):
        cols = pl.ds(t * rows, rows)

        def tops(i, carry):
            at = pl.ds(pl.multiple_of(i * rows, rows), rows)
            s = scores[at, cols]
            s0, s1 = s[:, :128], s[:, 128:]
            old = row_top[at, :]
            new = jnp.maximum(old, jnp.maximum(s0, s1))
            row_sum[at, :] = (
                row_sum[at, :] * jnp.exp(old - new) + jnp.exp(s0 - new) + jnp.exp(s1 - new)
            )
            row_top[at, :] = new
            return jnp.maximum(carry, jnp.max(s, axis=0, keepdims=True))

        ctop = lax.fori_loop(0, N_IMG, tops, jnp.full((1, rows), LOW, F32))

        def totals(i, carry):
            at = pl.ds(pl.multiple_of(i * rows, rows), rows)
            return carry + jnp.sum(jnp.exp(scores[at, cols] - ctop), axis=0, keepdims=True)

        csum = lax.fori_loop(0, N_IMG, totals, jnp.zeros((1, rows), F32))
        col_stat[t : t + 1, :] = ctop
        col_stat[N_TXT + t : N_TXT + t + 1, :] = csum

    def text_block(d, e):
        arrive(f"t{d}{e}", tx(d, e))
        txt_ready(2 * d + e, tx(d, e)[...])

    score_tiles(0, 0, 1)
    arrive("relay", relay_in, is0)
    send("t30", relay_in, tx(3, 0), relay_to, is0)
    send("t31", relay_in, tx(3, 1), relay_to.move(h=1), is0)
    arrive("i1", img_in.at[0])
    send("i3a", img_in.at[0, top], img_in.at[2, top], me.move(x=-1))
    arrive("i2", img_in.at[1])
    send("i3b", img_in.at[1, bottom], img_in.at[2, bottom], me.move(x=1))
    text_block(0, 1)
    send("t11", tx(0, 1), tx(1, 1), me.move(blk=-1), is1 | not0)
    send("t21", tx(0, 1), tx(2, 1), me.move(blk=-2), is1 & not0)
    text_block(1, 0)
    send("t20", tx(1, 0), tx(2, 0), me.move(c=1), is1)
    img_ready(1, img_in[0])
    img_ready(2, img_in[1])
    score_tiles(0, 1, 3)
    text_block(2, 0)
    send("t30", tx(2, 0), tx(3, 0), me.move(c=1), is1)
    score_tiles(1, 0, 3)
    score_tiles(2, 0, 3)
    score_tiles(4, 0, 3)
    arrive("i3a", img_in.at[2, top])
    arrive("i3b", img_in.at[2, bottom])
    img_ready(3, img_in[2])
    for t in (0, 1, 2, 4):
        score_tiles(t, 3, 4)
        block_stats(t)
    text_block(3, 0)
    score_tiles(6, 0, 4)
    block_stats(6)
    text_block(1, 1)
    send("t21", tx(1, 1), tx(2, 1), me.move(c=1), is1)
    score_tiles(3, 0, 4)
    block_stats(3)
    text_block(2, 1)
    send("t31", tx(2, 1), tx(3, 1), me.move(c=1), is1)
    score_tiles(5, 0, 4)
    block_stats(5)
    text_block(3, 1)
    score_tiles(7, 0, 4)
    block_stats(7)

    for n, (d, g) in enumerate(DELTAS):
        m = DELTAS.index((-d, g))
        send(f"c{m}", col_stat, col_got.at[m], me.move(blk=d, h=g))
    for i in range(N_IMG):
        at = pl.ds(i * rows, rows)
        m = jnp.transpose(row_top[at, :])
        s = jnp.transpose(row_sum[at, :])
        best = jnp.max(m, axis=0, keepdims=True)
        row_stat[i : i + 1, :] = best
        row_stat[N_IMG + i : N_IMG + i + 1, :] = jnp.sum(s * jnp.exp(m - best), axis=0, keepdims=True)
    for o in (1, 2, 3):
        send(f"r{4 - o}", row_stat, row_got.at[4 - o - 1], me.move(x=o))
    for n in range(len(DELTAS)):
        arrive(f"c{n}", col_got.at[n])
    for o in (1, 2, 3):
        arrive(f"r{o}", row_got.at[o - 1])

    def join(parts):
        best = functools.reduce(jnp.maximum, [m for m, _ in parts])
        return best + jnp.log(sum(s * jnp.exp(m - best) for m, s in parts))

    text_lse = []
    for t in range(N_TXT):
        d, e = t // 2, t % 2
        parts = [(col_stat[t : t + 1, :], col_stat[N_TXT + t : N_TXT + t + 1, :])]
        for n, (dd, g) in enumerate(DELTAS):
            if 0 <= d - dd < WINDOW:
                u = 2 * (d - dd) + (1 - e if g else e)
                parts.append((col_got[n, u : u + 1, :], col_got[n, N_TXT + u : N_TXT + u + 1, :]))
        text_lse.append(join(parts))
    loss_part = 0.5 * text_lse[0]
    for i in range(N_IMG):
        parts = [(row_stat[i : i + 1, :], row_stat[N_IMG + i : N_IMG + i + 1, :])]
        for o in (1, 2, 3):
            u = OFFSETS.index((OFFSETS[i] - o) % 4)
            parts.append((row_got[o - 1, u : u + 1, :], row_got[o - 1, N_IMG + u : N_IMG + u + 1, :]))
        lse = join(parts)
        if i == 0:
            loss_part += 0.5 * lse
        row_top[pl.ds(i * rows, rows), :] = jnp.transpose(jnp.broadcast_to(lse, (128, rows)))

    diagonal = lax.broadcasted_iota(jnp.int32, (rows, rows), 0) == lax.broadcasted_iota(
        jnp.int32, (rows, rows), 1
    )
    own = scores[pl.ds(0, rows), pl.ds(0, rows)]
    loss_part -= jnp.sum(jnp.where(diagonal, own, 0.0), axis=0, keepdims=True)
    scale_part = jnp.zeros((1, rows), F32)

    def weigh(t, scale_part):
        cols = pl.ds(t * rows, rows)

        def tile(i, carry):
            at = pl.ds(pl.multiple_of(i * rows, rows), rows)
            s = scores[at, cols]
            lse = row_top[at, :]
            by_row = jnp.exp(s - jnp.concatenate([lse, lse], axis=1))
            w = 0.5 * (by_row + jnp.exp(s - text_lse[t]))
            if t == 0:
                w = jnp.where(diagonal & (i == 0), w - 1.0, w)
            r_hi[at, cols], r_lo[at, cols] = split(w)
            return carry + jnp.sum(w * s, axis=0, keepdims=True)

        return lax.fori_loop(0, N_IMG, tile, scale_part)

    def text_partial(d, e):
        t = 2 * d + e
        cols = pl.ds(t * rows, rows)

        def part(n, carry):
            wide = pl.ds(pl.multiple_of(n * 256, 256), 256)
            acc = dot(r_hi[:, cols], img_hi[:, wide], tn)
            acc += dot(r_hi[:, cols], img_lo[:, wide], tn)
            acc += dot(r_lo[:, cols], img_hi[:, wide], tn)
            txt_part[t, :, wide] = acc
            return carry

        lax.fori_loop(0, img_ref.shape[1] // 256, part, 0)

    def image_partial(i):
        at = pl.ds(i * rows, rows)

        def part(n, carry):
            wide = pl.ds(pl.multiple_of(n * 256, 256), 256)
            acc = dot(r_hi[at, :], txt_hi[:, wide], nn)
            acc += dot(r_hi[at, :], txt_lo[:, wide], nn)
            acc += dot(r_lo[at, :], txt_hi[:, wide], nn)
            img_part[i, :, wide] = acc
            return carry

        lax.fori_loop(0, img_ref.shape[1] // 256, part, 0)

    def add(dst, src):
        dst[...] += src[...]

    def gp(d, e):
        return txt_part.at[2 * d + e]

    for t in (7, 6, 5, 4, 3, 2, 1, 0):
        scale_part = weigh(t, scale_part)

    at3 = me.z == 3

    def up(d, e, distance):
        if e == 0:
            send(f"a{e}", gp(d, e), ring_got.at[e], me.move(blk=distance), is1)
        else:
            send(f"a{e}", gp(d, e), ring_got.at[e], me.move(blk=distance), is1 & (me.z != 3))
            send(f"a{e}", gp(d, e), ring_got.at[e], me.move(blk=distance, h=1), is1 & at3)

    def chip(d, e):
        send(f"g{d}{e}", gp(d + 1, e), chip_got.at[2 * d + e], me.move(c=1), is0)

    def chip_add(d, e):
        @pl.when(is1)
        def _():
            copy(f"g{d}{e}", gp(d, e), chip_got.at[2 * d + e], me.move(c=1)).wait_recv()
            add(gp(d, e), chip_got.at[2 * d + e])

    for e in (1, 0):
        text_partial(3, e)
        chip(2, e)
        send(f"b{e}", gp(3, e), relay_got.at[e], relay_from.move(h=e), is1)
    for e in (1, 0):
        text_partial(2, e)
        chip(1, e)
        chip_add(2, e)
        up(2, e, 2)
    image_partial(3)
    send("p3a", img_part.at[3, top], img_half.at[0], me.move(x=1))
    send("p3b", img_part.at[3, bottom], img_half.at[1], me.move(x=-1))
    for e in (1, 0):
        text_partial(1, e)
        chip(0, e)
        chip_add(1, e)
        up(1, e, 1)
    image_partial(1)
    send("p1b", img_part.at[1, bottom], img_got.at[0, bottom], me.move(x=1))
    image_partial(2)
    send("p2a", img_part.at[2, top], img_got.at[1, top], me.move(x=-1))

    @pl.when(is0)
    def _():
        copy("b0", relay_got.at[0], relay_got.at[0], me.move(h=1)).wait_recv()
        copy("b1", relay_got.at[1], relay_got.at[1], me.move(h=1)).wait_recv()
        add(relay_got.at[0], relay_got.at[1])

    send("back", relay_got.at[0], relay_back, me.move(z=-1), is0)
    text_partial(0, 1)
    arrive("p3a", img_half.at[0])
    add(img_part.at[1, top], img_half.at[0])
    send("p1a", img_part.at[1, top], img_got.at[0, top], me.move(x=1))
    arrive("p3b", img_half.at[1])
    add(img_part.at[2, bottom], img_half.at[1])
    send("p2b", img_part.at[2, bottom], img_got.at[1, bottom], me.move(x=-1))
    chip_add(0, 1)
    arrive("a1", ring_got.at[1])

    @pl.when(not0)
    def _():
        add(gp(0, 1), ring_got.at[1])

    send("y", gp(0, 1), pair_got, me.move(h=1))
    text_partial(0, 0)
    chip_add(0, 0)

    @pl.when(at0)
    def _():
        add(gp(0, 0), ring_got.at[1])

    image_partial(0)

    loss_sum = jnp.sum(loss_part, axis=1, keepdims=True)
    scale_sum = jnp.sum(scale_part, axis=1, keepdims=True) / scale
    line = lax.broadcasted_iota(jnp.int32, (8, 128), 0)
    total = jnp.where(line == 0, loss_sum, scale_sum)
    stages = [
        [me.move(c=1)],
        [me.move(h=1)],
        [me.move(yl=1)],
        [me.move(x=1), me.move(x=2), me.move(x=3)],
        [me.move(z=1), me.move(z=2), me.move(z=3)],
    ]
    n = 0
    for level, peers in enumerate(stages):
        sum_send[level] = total
        for j, p in enumerate(peers):
            send(f"s{n + j}", sum_send.at[level], sum_got.at[n + j], p)
        for j in range(len(peers)):
            arrive(f"s{n + j}", sum_got.at[n + j])
            total = total + sum_got[n + j]
        n += len(peers)
    pairs = rows * lax.axis_size("blk") * lax.axis_size("row")
    sums_ref[...] = total / pairs

    arrive("a0", ring_got.at[0])
    arrive("back", relay_back, is0)

    @pl.when(is0)
    def _():
        add(gp(0, 0), relay_back)

    for name, at, j in (("p1b", bottom, 0), ("p2a", top, 1), ("p1a", top, 0), ("p2b", bottom, 1)):
        arrive(name, img_got.at[j, at])
    img_out[...] = scale * (img_part[0] + img_got[0] + img_got[1])
    arrive("y", pair_got)
    txt_out[...] = scale * (txt_part[0] + ring_got[0] + pair_got[...])

    for c, when in pending:
        if when is None:
            c.wait_send()
        else:
            pl.when(when)(c.wait_send)


N_SEM = 80


def shards(image_embed, text_embed, logit_scale):
    rows, width = image_embed.shape
    block = (rows, width)
    vmem = pl.BlockSpec(memory_space=pltpu.VMEM)
    sums, image_grad, text_grad = pl.pallas_call(
        functools.partial(kernel, rows),
        out_shape=(
            jax.ShapeDtypeStruct((8, 128), F32),
            jax.ShapeDtypeStruct(block, F32),
            jax.ShapeDtypeStruct(block, F32),
        ),
        in_specs=[pl.BlockSpec(memory_space=pltpu.SMEM), vmem, vmem],
        out_specs=(vmem, vmem, vmem),
        scratch_shapes=[
            pltpu.VMEM((3, *block), F32),
            pltpu.VMEM((7, *block), F32),
            pltpu.VMEM(block, F32),
            pltpu.VMEM((N_IMG * rows, width), BF16),
            pltpu.VMEM((N_IMG * rows, width), BF16),
            pltpu.VMEM((N_TXT * rows, width), BF16),
            pltpu.VMEM((N_TXT * rows, width), BF16),
            pltpu.VMEM((N_IMG * rows, N_TXT * rows), F32),
            pltpu.VMEM((N_IMG * rows, N_TXT * rows), BF16),
            pltpu.VMEM((N_IMG * rows, N_TXT * rows), BF16),
            pltpu.VMEM((N_IMG * rows, 128), F32),
            pltpu.VMEM((N_IMG * rows, 128), F32),
            pltpu.VMEM((2 * N_IMG, rows), F32),
            pltpu.VMEM((2 * N_TXT, rows), F32),
            pltpu.VMEM((3, 2 * N_IMG, rows), F32),
            pltpu.VMEM((len(DELTAS), 2 * N_TXT, rows), F32),
            pltpu.VMEM((N_IMG, *block), F32),
            pltpu.VMEM((N_TXT, *block), F32),
            pltpu.VMEM((6, *block), F32),
            pltpu.VMEM((2, *block), F32),
            pltpu.VMEM((2, *block), F32),
            pltpu.VMEM(block, F32),
            pltpu.VMEM(block, F32),
            pltpu.VMEM((2, *block), F32),
            pltpu.VMEM((2, rows // 2, width), F32),
            pltpu.VMEM((5, 8, 128), F32),
            pltpu.VMEM((9, 8, 128), F32),
            pltpu.SemaphoreType.DMA((N_SEM,)),
            pltpu.SemaphoreType.DMA((N_SEM,)),
        ],
        compiler_params=pltpu.CompilerParams(
            collective_id=0, has_side_effects=True, vmem_limit_bytes=62 << 20
        ),
        cost_estimate=pl.CostEstimate(flops=29 * 10**9, bytes_accessed=4 * 10**6, transcendentals=10**7),
    )(logit_scale, image_embed, text_embed)
    return sums[0, :1], sums[1, :1], image_grad, text_grad


def solution(mesh):
    in_specs = (P(("blk", "row"), None), P(("blk", "row"), None), P())
    out_specs = (P(), P(), P(("blk", "row"), None), P(("blk", "row"), None))
    return jax.shard_map(shards, mesh=mesh, in_specs=in_specs, out_specs=out_specs, check_vma=False)
```

time: 455 us -> 174 us (0.38); the launches traced: 448 us -> 174 us
  Pallas kernels: 0 us -> 168 us
  waiting for transfers between devices: 156 us -> 0 us
  matrix products: 118 us -> 0 us
  blocking collectives: 98.3 us -> 0 us
  starting transfers between devices: 40.1 us -> 0 us
  between operations: 23.9 us -> 1.29 us
  other arithmetic: 9.85 us -> 0 us
    pallas_call x0 -> x1, Pallas kernels: none -> 168 us  [shards(): pl.pallas_call(functools.partial(kernel, rows), out_shape=(jax.ShapeDtype...]
    dot_general x15 -> x0, matrix products: 118 us -> none  [the longest x7 53.3 us: raw_scores(): lax.dot_general(group_imgs, text_block, (((1,), (1,)), ((), ())), precisi...]
    ppermute x18 -> x0, waiting for transfers between devices: 89.4 us -> none  [from_behind(): return lax.ppermute(block, axis, route)]
    psum x2 -> x0, blocking collectives: 81.5 us -> none  [the longest x1 64.4 us: shards(): loss_sum, scale_total = lax.psum((loss_term, scale_term), ('blk', 'row'))]
    reduce_scatter x1 -> x0, waiting for transfers between devices: 56 us -> none  [shards(): lax.psum_scatter(image_part, 'row', scatter_dimension=0, tiled=True)]
    ppermute x18 -> x0, starting transfers between devices: 40 us -> none  [from_behind(): return lax.ppermute(block, axis, route)]
    pmax x1 -> x0, blocking collectives: 16.8 us -> none  [shards(): group_top = lax.pmax(row_top, 'row')]
    all_gather x1 -> x0, waiting for transfers between devices: 10.1 us -> none  [shards(): group_imgs = lax.all_gather(image_embed, 'row', axis=0, tiled=True)]
  transfers between devices with their start and end apart: 20 -> 0, of which waited for: 11 -> 0; matrix products, arithmetic and copies ran while one was open for 22% -> 0% of each run, Pallas kernels for 0% -> 0%
where the time goes in v1:
time: 174 us
  Pallas kernels  168 us (97%)
  local copies, waits for them, and re-layouts  4.29 us (2%)
    pallas_call x1, Pallas kernels, shards(): pl.pallas_call(functools.partial(kernel, rows), out_shape=(jax.ShapeDtype...  168 us

profile of v1, /device:TPU:9, one launch (start us, length us, event | category | flops | bytes accessed | tf_op | source)
XLA Modules:
  0.0 173.6 jit_solution(16935274017250637072)
XLA Ops:
  1.3 168.0 %shard_map.66 = (f32[8,128]{1,0:T(8,128)}, f32[256,768]{1,0:T(8,128)}, f32[256,768]{1,0:T(8,128)}) custom-call(f32[1]{0:T(128)S(6)} %copy.9.scale_ref, f32[256,768]{1,0:T(8,128)} %img_ref.1, f32[256,768]{1,0:T(8,128)} %txt_ref.1), custom_call_target="tpu_custom_call" | custom-call | flops 28999999488 | bytes 4000000 | tf_op jit(solution)/shard_map/pallas_call | solution.py:491
  169.3 1.3 fusion
  170.6 0.0 copy-start
  170.6 2.1 %copy.10 = f32[256,768]{1,0:T(8,128)} copy(f32[256,768]{1,0:T(8,128)} %get-tuple-element.18) | data formatting | bytes 1572864
  172.7 0.0 copy-done
  172.7 0.9 copy.11
Async XLA Ops:
  170.6 2.1 %copy-start = (f32[256,768]{1,0:T(8,128)S(1)}, f32[256,768]{1,0:T(8,128)}, u32[]{:S(2)}) copy-start(f32[256,768]{1,0:T(8,128)} %get-tuple-element.19) | copy-start | bytes 2359300

commit v2 on v1

--- a/solution.py
+++ b/solution.py
@@ -129,15 +129,23 @@
         else:
             pl.when(when)(c.wait_recv)
 
-    source_plane_from_relay = me.move(z=-1)
-    relay_to = source_plane_from_relay.move(plane=-2)
-    relay_to = Place(relay_to.y_lo, relay_to.z, 1 - me.core, me.y_hi, me.x)
-    relay_from = me.move(plane=2).move(z=1)
-    relay_from = Place(relay_from.y_lo, relay_from.z, 1 - me.core, me.y_hi, me.x)
+    def pieces(name, src, dst, place, when=None):
+        send(name + "a", src.at[top], dst.at[top], place, when)
+        send(name + "b", src.at[bottom], dst.at[bottom], place, when)
+
+    def arrive_pieces(name, dst, when=None):
+        arrive(name + "a", dst.at[top], when)
+        arrive(name + "b", dst.at[bottom], when)
+
+    relay_to = me.move(z=-1).move(plane=-2).move(c=1)
+    relay_from = me.move(plane=2).move(z=1).move(c=1)
+    back_to = me.move(z=1).move(plane=2).move(c=1)
+    back_from = me.move(plane=-2).move(z=-1).move(c=1)
+    crossing = (me.z == 1) | (me.z == 2)
 
     partners = [me.move(x=1), me.move(x=2), me.move(x=3), me.move(h=1), me.move(c=1)]
     partners += [me.move(z=1), me.move(z=2), me.move(z=3), me.move(yl=1)]
-    partners += [relay_to, relay_to.move(h=1), relay_from, relay_from.move(h=1)]
+    partners += [relay_from, relay_from.move(h=1), back_from, back_from.move(h=1)]
     partners += [me.move(blk=d, h=g) for d, g in DELTAS if d != 0]
     barrier = pltpu.get_barrier_semaphore()
     for p in partners:
@@ -150,14 +158,16 @@
     at0 = me.z == 0
     not0 = me.z != 0
     prev = [me.move(blk=-1), me.move(blk=-2)]
-    send("i1", img_ref, img_in.at[0], me.move(x=-1))
-    send("i2", img_ref, img_in.at[1], me.move(x=1))
-    send("t01", txt_ref, tx(0, 1), me.move(h=1))
-    send("t10", txt_ref, tx(1, 0), me.move(blk=-1))
-    send("t20", txt_ref, tx(2, 0), me.move(blk=-2), is1)
-    send("relay", txt_ref, relay_in, me.move(z=1), is0)
-    send("t11", txt_ref, tx(1, 1), me.move(blk=-1, h=1), is0 & at0)
-    send("t21", txt_ref, tx(2, 1), me.move(blk=-2, h=1), is1 & at0)
+    at3 = me.z == 3
+    pieces("t10", txt_ref, tx(1, 0), me.move(blk=-1), is1 | not0)
+    early = len(pending)
+    pieces("t10", txt_ref, tx(1, 0), me.move(blk=-1), is0 & at0)
+    pieces("t20", txt_ref, tx(2, 0), me.move(blk=-2), is1 & at0)
+    pieces("t20", txt_ref, tx(2, 0), me.move(blk=-2), is1 & not0)
+    pieces("r0", txt_ref, relay_in.at[0], me.move(z=1), is0)
+    pieces("t01", txt_ref, tx(0, 1), me.move(h=1), not0)
+    pieces("i1", img_ref, img_in.at[0], me.move(x=-1))
+    pieces("i2", img_ref, img_in.at[1], me.move(x=1))
 
     def img_ready(i, value):
         high, low = split(value)
@@ -194,7 +204,7 @@
             scores[at, cols] = scale * raw
             return carry
 
-        lax.fori_loop(first, last, tile, 0)
+        lax.fori_loop(first, last, tile, 0, unroll=True)
 
     def block_stats(t):
         cols = pl.ds(t * rows, rows)
@@ -211,61 +221,78 @@
             row_top[at, :] = new
             return jnp.maximum(carry, jnp.max(s, axis=0, keepdims=True))
 
-        ctop = lax.fori_loop(0, N_IMG, tops, jnp.full((1, rows), LOW, F32))
+        ctop = lax.fori_loop(0, N_IMG, tops, jnp.full((1, rows), LOW, F32), unroll=True)
 
         def totals(i, carry):
             at = pl.ds(pl.multiple_of(i * rows, rows), rows)
             return carry + jnp.sum(jnp.exp(scores[at, cols] - ctop), axis=0, keepdims=True)
 
-        csum = lax.fori_loop(0, N_IMG, totals, jnp.zeros((1, rows), F32))
+        csum = lax.fori_loop(0, N_IMG, totals, jnp.zeros((1, rows), F32), unroll=True)
         col_stat[t : t + 1, :] = ctop
         col_stat[N_TXT + t : N_TXT + t + 1, :] = csum
 
     def text_block(d, e):
-        arrive(f"t{d}{e}", tx(d, e))
+        arrive_pieces(f"t{d}{e}", tx(d, e))
         txt_ready(2 * d + e, tx(d, e)[...])
 
+    def scored(t):
+        score_tiles(t, 0, N_IMG)
+        block_stats(t)
+
     score_tiles(0, 0, 1)
-    arrive("relay", relay_in, is0)
-    send("t30", relay_in, tx(3, 0), relay_to, is0)
-    send("t31", relay_in, tx(3, 1), relay_to.move(h=1), is0)
-    arrive("i1", img_in.at[0])
+    for p, at in (("a", top), ("b", bottom)):
+        arrive("r0" + p, relay_in.at[0, at], is0)
+        send("t30" + p, relay_in.at[0, at], tx(3, 0).at[at], relay_to, is0)
+        send("t31" + p, relay_in.at[0, at], tx(3, 1).at[at], relay_to.move(h=1), is0 & crossing)
+    for i in range(early, early + 4):
+        c, when = pending[i]
+        pl.when(when)(c.wait_send)
+        pending[i] = None
+    pieces("t01", txt_ref, tx(0, 1), me.move(h=1), at0)
+    for p, at in (("a", top), ("b", bottom)):
+        arrive("t01" + p, tx(0, 1).at[at])
+        send("t11" + p, tx(0, 1).at[at], tx(1, 1).at[at], me.move(blk=-1), is1 | not0)
+        send("t21" + p, tx(0, 1).at[at], tx(2, 1).at[at], me.move(blk=-2), is1 & not0)
+        send("r1" + p, tx(0, 1).at[at], relay_in.at[1, at], me.move(z=1), is0 & (me.z >= 2))
+    arrive("i1a", img_in.at[0, top])
     send("i3a", img_in.at[0, top], img_in.at[2, top], me.move(x=-1))
-    arrive("i2", img_in.at[1])
+    arrive("i2b", img_in.at[1, bottom])
     send("i3b", img_in.at[1, bottom], img_in.at[2, bottom], me.move(x=1))
-    text_block(0, 1)
-    send("t11", tx(0, 1), tx(1, 1), me.move(blk=-1), is1 | not0)
-    send("t21", tx(0, 1), tx(2, 1), me.move(blk=-2), is1 & not0)
-    text_block(1, 0)
-    send("t20", tx(1, 0), tx(2, 0), me.move(c=1), is1)
+    txt_ready(1, tx(0, 1)[...])
+    score_tiles(1, 0, 1)
+    for d in (1, 2):
+        for p, at in (("a", top), ("b", bottom)):
+            arrive(f"t{d}0{p}", tx(d, 0).at[at])
+            send(f"t{d + 1}0{p}", tx(d, 0).at[at], tx(d + 1, 0).at[at], me.move(c=1), is1)
+            send(f"t{d}1{p}", tx(d, 0).at[at], tx(d, 1).at[at], me.move(h=1), is1 & at3)
+        txt_ready(2 * d, tx(d, 0)[...])
+    arrive("i1b", img_in.at[0, bottom])
+    arrive("i2a", img_in.at[1, top])
     img_ready(1, img_in[0])
     img_ready(2, img_in[1])
     score_tiles(0, 1, 3)
-    text_block(2, 0)
-    send("t30", tx(2, 0), tx(3, 0), me.move(c=1), is1)
-    score_tiles(1, 0, 3)
-    score_tiles(2, 0, 3)
-    score_tiles(4, 0, 3)
+    score_tiles(1, 1, 3)
+    for p, at in (("a", top), ("b", bottom)):
+        arrive("r1" + p, relay_in.at[1, at], is0 & ~crossing)
+        send("t31" + p, relay_in.at[1, at], tx(3, 1).at[at], relay_to, is0 & ~crossing)
     arrive("i3a", img_in.at[2, top])
     arrive("i3b", img_in.at[2, bottom])
     img_ready(3, img_in[2])
-    for t in (0, 1, 2, 4):
+    for t in (0, 1):
         score_tiles(t, 3, 4)
         block_stats(t)
+    scored(2)
+    scored(4)
     text_block(3, 0)
-    score_tiles(6, 0, 4)
-    block_stats(6)
+    scored(6)
     text_block(1, 1)
-    send("t21", tx(1, 1), tx(2, 1), me.move(c=1), is1)
-    score_tiles(3, 0, 4)
-    block_stats(3)
+    pieces("t21", tx(1, 1), tx(2, 1), me.move(c=1), is1)
     text_block(2, 1)
-    send("t31", tx(2, 1), tx(3, 1), me.move(c=1), is1)
-    score_tiles(5, 0, 4)
-    block_stats(5)
+    pieces("t31", tx(2, 1), tx(3, 1), me.move(c=1), is1)
+    scored(3)
+    scored(5)
     text_block(3, 1)
-    score_tiles(7, 0, 4)
-    block_stats(7)
+    scored(7)
 
     for n, (d, g) in enumerate(DELTAS):
         m = DELTAS.index((-d, g))
@@ -329,7 +356,7 @@
             r_hi[at, cols], r_lo[at, cols] = split(w)
             return carry + jnp.sum(w * s, axis=0, keepdims=True)
 
-        return lax.fori_loop(0, N_IMG, tile, scale_part)
+        return lax.fori_loop(0, N_IMG, tile, scale_part, unroll=True)
 
     def text_partial(d, e):
         t = 2 * d + e
@@ -367,74 +394,95 @@
     for t in (7, 6, 5, 4, 3, 2, 1, 0):
         scale_part = weigh(t, scale_part)
 
-    at3 = me.z == 3
-
     def up(d, e, distance):
         if e == 0:
-            send(f"a{e}", gp(d, e), ring_got.at[e], me.move(blk=distance), is1)
+            pieces(f"a{e}", gp(d, e), ring_got.at[e], me.move(blk=distance), is1)
         else:
-            send(f"a{e}", gp(d, e), ring_got.at[e], me.move(blk=distance), is1 & (me.z != 3))
-            send(f"a{e}", gp(d, e), ring_got.at[e], me.move(blk=distance, h=1), is1 & at3)
+            pieces(f"a{e}", gp(d, e), ring_got.at[e], me.move(blk=distance), is1 & (me.z != 3))
+            pieces(f"a{e}", gp(d, e), ring_got.at[e], me.move(blk=distance, h=1), is1 & at3)
 
     def chip(d, e):
         send(f"g{d}{e}", gp(d + 1, e), chip_got.at[2 * d + e], me.move(c=1), is0)
 
     def chip_add(d, e):
+        arrive(f"g{d}{e}", chip_got.at[2 * d + e], is1)
+
         @pl.when(is1)
         def _():
-            copy(f"g{d}{e}", gp(d, e), chip_got.at[2 * d + e], me.move(c=1)).wait_recv()
             add(gp(d, e), chip_got.at[2 * d + e])
 
-    for e in (1, 0):
-        text_partial(3, e)
-        chip(2, e)
-        send(f"b{e}", gp(3, e), relay_got.at[e], relay_from.move(h=e), is1)
-    for e in (1, 0):
-        text_partial(2, e)
-        chip(1, e)
-        chip_add(2, e)
-        up(2, e, 2)
+    def forward(e):
+        for p, at in (("a", top), ("b", bottom)):
+            arrive(f"b{e}{p}", relay_got.at[e, at], is1)
+            if e == 0:
+                send(f"back{e}{p}", relay_got.at[e, at], relay_back.at[e, at], back_to, is1)
+            else:
+                send(f"back{e}{p}", relay_got.at[e, at], relay_back.at[e, at], back_to, is1 & ~crossing)
+                send(f"back{e}{p}", relay_got.at[e, at], relay_back.at[e, at], back_to.move(h=1), is1 & crossing)
+
+    text_partial(3, 1)
+    chip(2, 1)
+    pieces("b1", gp(3, 1), relay_got.at[1], me.move(z=-1), is1)
+    text_partial(2, 1)
+    chip(1, 1)
+    chip_add(2, 1)
+    up(2, 1, 2)
+    text_partial(1, 1)
+    chip(0, 1)
+    chip_add(1, 1)
+    up(1, 1, 1)
     image_partial(3)
     send("p3a", img_part.at[3, top], img_half.at[0], me.move(x=1))
     send("p3b", img_part.at[3, bottom], img_half.at[1], me.move(x=-1))
-    for e in (1, 0):
-        text_partial(1, e)
-        chip(0, e)
-        chip_add(1, e)
-        up(1, e, 1)
+    text_partial(3, 0)
+    chip(2, 0)
+    pieces("b0", gp(3, 0), relay_got.at[0], me.move(z=-1), is1)
+    forward(1)
     image_partial(1)
     send("p1b", img_part.at[1, bottom], img_got.at[0, bottom], me.move(x=1))
     image_partial(2)
     send("p2a", img_part.at[2, top], img_got.at[1, top], me.move(x=-1))
-
-    @pl.when(is0)
-    def _():
-        copy("b0", relay_got.at[0], relay_got.at[0], me.move(h=1)).wait_recv()
-        copy("b1", relay_got.at[1], relay_got.at[1], me.move(h=1)).wait_recv()
-        add(relay_got.at[0], relay_got.at[1])
-
-    send("back", relay_got.at[0], relay_back, me.move(z=-1), is0)
-    text_partial(0, 1)
+    text_partial(2, 0)
+    chip(1, 0)
+    chip_add(2, 0)
+    up(2, 0, 2)
     arrive("p3a", img_half.at[0])
     add(img_part.at[1, top], img_half.at[0])
     send("p1a", img_part.at[1, top], img_got.at[0, top], me.move(x=1))
     arrive("p3b", img_half.at[1])
     add(img_part.at[2, bottom], img_half.at[1])
     send("p2b", img_part.at[2, bottom], img_got.at[1, bottom], me.move(x=-1))
+    text_partial(1, 0)
+    chip(0, 0)
+    chip_add(1, 0)
+    up(1, 0, 1)
+    text_partial(0, 1)
     chip_add(0, 1)
-    arrive("a1", ring_got.at[1])
-
-    @pl.when(not0)
-    def _():
-        add(gp(0, 1), ring_got.at[1])
-
-    send("y", gp(0, 1), pair_got, me.move(h=1))
+    forward(0)
+    for p, at in (("a", top), ("b", bottom)):
+        arrive("a1" + p, ring_got.at[1, at])
+
+        @pl.when(not0)
+        def _(at=at):
+            add(gp(0, 1).at[at], ring_got.at[1, at])
+
+        arrive("back1" + p, relay_back.at[1, at], is0)
+
+        @pl.when(is0 & (me.z >= 2))
+        def _(at=at):
+            add(gp(0, 1).at[at], relay_back.at[1, at])
+
+        send("y" + p, gp(0, 1).at[at], pair_got.at[at], me.move(h=1))
     text_partial(0, 0)
     chip_add(0, 0)
 
     @pl.when(at0)
     def _():
         add(gp(0, 0), ring_got.at[1])
+
+    @pl.when(is0 & (me.z < 2))
+    def _():
+        add(gp(0, 0), relay_back.at[1])
 
     image_partial(0)
 
@@ -461,27 +509,27 @@
     pairs = rows * lax.axis_size("blk") * lax.axis_size("row")
     sums_ref[...] = total / pairs
 
-    arrive("a0", ring_got.at[0])
-    arrive("back", relay_back, is0)
+    arrive_pieces("a0", ring_got.at[0])
+    arrive_pieces("back0", relay_back.at[0], is0)
 
     @pl.when(is0)
     def _():
-        add(gp(0, 0), relay_back)
+        add(gp(0, 0), relay_back.at[0])
 
     for name, at, j in (("p1b", bottom, 0), ("p2a", top, 1), ("p1a", top, 0), ("p2b", bottom, 1)):
         arrive(name, img_got.at[j, at])
     img_out[...] = scale * (img_part[0] + img_got[0] + img_got[1])
-    arrive("y", pair_got)
+    arrive_pieces("y", pair_got)
     txt_out[...] = scale * (txt_part[0] + ring_got[0] + pair_got[...])
 
-    for c, when in pending:
+    for c, when in [entry for entry in pending if entry is not None]:
         if when is None:
             c.wait_send()
         else:
             pl.when(when)(c.wait_send)
 
 
-N_SEM = 80
+N_SEM = 128
 
 
 def shards(image_embed, text_embed, logit_scale):
@@ -500,7 +548,7 @@
         scratch_shapes=[
             pltpu.VMEM((3, *block), F32),
             pltpu.VMEM((7, *block), F32),
-            pltpu.VMEM(block, F32),
+            pltpu.VMEM((2, *block), F32),
             pltpu.VMEM((N_IMG * rows, width), BF16),
             pltpu.VMEM((N_IMG * rows, width), BF16),
             pltpu.VMEM((N_TXT * rows, width), BF16),
@@ -519,7 +567,7 @@
             pltpu.VMEM((6, *block), F32),
             pltpu.VMEM((2, *block), F32),
             pltpu.VMEM((2, *block), F32),
-            pltpu.VMEM(block, F32),
+            pltpu.VMEM((2, *block), F32),
             pltpu.VMEM(block, F32),
             pltpu.VMEM((2, *block), F32),
             pltpu.VMEM((2, rows // 2, width), F32),

time: 174 us -> 154 us (0.89)
  Pallas kernels: 168 us -> 148 us
    pallas_call x1, Pallas kernels: 168 us -> 148 us  [shards(): pl.pallas_call(functools.partial(kernel, rows), out_shape=(jax.ShapeDtype...]
where the time goes in v2:
time: 154 us; the launch traced here: 153 us
  Pallas kernels  148 us (96%)
  local copies, waits for them, and re-layouts  4.29 us (3%)
    pallas_call x1, Pallas kernels, shards(): pl.pallas_call(functools.partial(kernel, rows), out_shape=(jax.ShapeDtype...  148 us

profile of v2, /device:TPU:9, one launch (start us, length us, event | category | flops | bytes accessed | tf_op | source)
XLA Modules:
  0.0 153.3 jit_solution(11038030757117647370)
XLA Ops:
  1.3 147.8 %shard_map.66 = (f32[8,128]{1,0:T(8,128)}, f32[256,768]{1,0:T(8,128)}, f32[256,768]{1,0:T(8,128)}) custom-call(f32[1]{0:T(128)S(6)} %copy.9.scale_ref, f32[256,768]{1,0:T(8,128)} %img_ref.1, f32[256,768]{1,0:T(8,128)} %txt_ref.1), custom_call_target="tpu_custom_call" | custom-call | flops 28999999488 | bytes 4000000 | tf_op jit(solution)/shard_map/pallas_call | solution.py:539
  149.0 1.3 fusion
  150.3 0.0 copy-start
  150.3 2.1 %copy.10 = f32[256,768]{1,0:T(8,128)} copy(f32[256,768]{1,0:T(8,128)} %get-tuple-element.18) | data formatting | bytes 1572864
  152.5 0.0 copy-done
  152.5 0.9 copy.11
Async XLA Ops:
  150.3 2.1 %copy-start = (f32[256,768]{1,0:T(8,128)S(1)}, f32[256,768]{1,0:T(8,128)}, u32[]{:S(2)}) copy-start(f32[256,768]{1,0:T(8,128)} %get-tuple-element.19) | copy-start | bytes 2359300

commit v3 on v2

--- a/solution.py
+++ b/solution.py
@@ -79,7 +79,6 @@
     col_stat,
     row_got,
     col_got,
-    img_part,
     txt_part,
     chip_got,
     ring_got,
@@ -145,7 +144,7 @@
 
     partners = [me.move(x=1), me.move(x=2), me.move(x=3), me.move(h=1), me.move(c=1)]
     partners += [me.move(z=1), me.move(z=2), me.move(z=3), me.move(yl=1)]
-    partners += [relay_from, relay_from.move(h=1), back_from, back_from.move(h=1)]
+    partners += [me.move(z=-1, c=1), relay_from, relay_from.move(h=1), back_from, back_from.move(h=1)]
     partners += [me.move(blk=d, h=g) for d, g in DELTAS if d != 0]
     barrier = pltpu.get_barrier_semaphore()
     for p in partners:
@@ -362,15 +361,10 @@
         t = 2 * d + e
         cols = pl.ds(t * rows, rows)
 
-        def part(n, carry):
-            wide = pl.ds(pl.multiple_of(n * 256, 256), 256)
-            acc = dot(r_hi[:, cols], img_hi[:, wide], tn)
-            acc += dot(r_hi[:, cols], img_lo[:, wide], tn)
-            acc += dot(r_lo[:, cols], img_hi[:, wide], tn)
-            txt_part[t, :, wide] = acc
-            return carry
-
-        lax.fori_loop(0, img_ref.shape[1] // 256, part, 0)
+        acc = dot(r_hi[:, cols], img_hi[...], tn)
+        acc += dot(r_hi[:, cols], img_lo[...], tn)
+        acc += dot(r_lo[:, cols], img_hi[...], tn)
+        txt_part[t] = acc
 
     def image_partial(i):
         at = pl.ds(i * rows, rows)
@@ -380,7 +374,7 @@
             acc = dot(r_hi[at, :], txt_hi[:, wide], nn)
             acc += dot(r_hi[at, :], txt_lo[:, wide], nn)
             acc += dot(r_lo[at, :], txt_hi[:, wide], nn)
-            img_part[i, :, wide] = acc
+            scores[at, wide] = acc
             return carry
 
         lax.fori_loop(0, img_ref.shape[1] // 256, part, 0)
@@ -388,6 +382,9 @@
     def add(dst, src):
         dst[...] += src[...]
 
+    def held(i, at):
+        return scores.at[pl.ds(i * rows + at.start, at.size), pl.ds(0, img_ref.shape[1])]
+
     def gp(d, e):
         return txt_part.at[2 * d + e]
 
@@ -395,11 +392,23 @@
         scale_part = weigh(t, scale_part)
 
     def up(d, e, distance):
-        if e == 0:
-            pieces(f"a{e}", gp(d, e), ring_got.at[e], me.move(blk=distance), is1)
+        pieces(f"a{e}", gp(d, e), ring_got.at[e], me.move(blk=distance), is1 & (me.z != 3))
+        if e == 1:
+            pieces(f"q{d}", gp(d, 1), relay_back.at[d - 1], me.move(h=1), is1 & at3)
         else:
-            pieces(f"a{e}", gp(d, e), ring_got.at[e], me.move(blk=distance), is1 & (me.z != 3))
-            pieces(f"a{e}", gp(d, e), ring_got.at[e], me.move(blk=distance, h=1), is1 & at3)
+            for p, at in (("a", top), ("b", bottom)):
+                arrive(f"q{d}{p}", relay_back.at[d - 1, at], is1 & at3)
+
+                @pl.when(is1 & at3)
+                def _(at=at):
+                    add(gp(d, 0).at[at], relay_back.at[d - 1, at])
+
+                place = me.move(z=1) if d == 2 else me.move(z=1, c=1)
+                send("a1" + p, gp(d, 0).at[at], ring_got.at[1, at], place, is1 & at3)
+
+    def cross(p, at):
+        arrive("a1" + p, ring_got.at[1, at], at0)
+        send("a0" + p, ring_got.at[1, at], ring_got.at[0, at], me.move(yl=1), at0)
 
     def chip(d, e):
         send(f"g{d}{e}", gp(d + 1, e), chip_got.at[2 * d + e], me.move(c=1), is0)
@@ -431,36 +440,37 @@
     chip(0, 1)
     chip_add(1, 1)
     up(1, 1, 1)
+    text_partial(0, 1)
+    chip_add(0, 1)
+    pieces("y", gp(0, 1), pair_got, me.move(h=1), at0)
     image_partial(3)
-    send("p3a", img_part.at[3, top], img_half.at[0], me.move(x=1))
-    send("p3b", img_part.at[3, bottom], img_half.at[1], me.move(x=-1))
+    send("p3a", held(3, top), img_half.at[0], me.move(x=1))
+    send("p3b", held(3, bottom), img_half.at[1], me.move(x=-1))
     text_partial(3, 0)
     chip(2, 0)
     pieces("b0", gp(3, 0), relay_got.at[0], me.move(z=-1), is1)
     forward(1)
     image_partial(1)
-    send("p1b", img_part.at[1, bottom], img_got.at[0, bottom], me.move(x=1))
+    send("p1b", held(1, bottom), img_got.at[0, bottom], me.move(x=1))
     image_partial(2)
-    send("p2a", img_part.at[2, top], img_got.at[1, top], me.move(x=-1))
+    send("p2a", held(2, top), img_got.at[1, top], me.move(x=-1))
     text_partial(2, 0)
     chip(1, 0)
     chip_add(2, 0)
     up(2, 0, 2)
     arrive("p3a", img_half.at[0])
-    add(img_part.at[1, top], img_half.at[0])
-    send("p1a", img_part.at[1, top], img_got.at[0, top], me.move(x=1))
+    add(held(1, top), img_half.at[0])
+    send("p1a", held(1, top), img_got.at[0, top], me.move(x=1))
     arrive("p3b", img_half.at[1])
-    add(img_part.at[2, bottom], img_half.at[1])
-    send("p2b", img_part.at[2, bottom], img_got.at[1, bottom], me.move(x=-1))
+    add(held(2, bottom), img_half.at[1])
+    send("p2b", held(2, bottom), img_got.at[1, bottom], me.move(x=-1))
     text_partial(1, 0)
     chip(0, 0)
     chip_add(1, 0)
     up(1, 0, 1)
-    text_partial(0, 1)
-    chip_add(0, 1)
     forward(0)
     for p, at in (("a", top), ("b", bottom)):
-        arrive("a1" + p, ring_got.at[1, at])
+        arrive("a1" + p, ring_got.at[1, at], not0)
 
         @pl.when(not0)
         def _(at=at):
@@ -472,13 +482,11 @@
         def _(at=at):
             add(gp(0, 1).at[at], relay_back.at[1, at])
 
-        send("y" + p, gp(0, 1).at[at], pair_got.at[at], me.move(h=1))
+        send("y" + p, gp(0, 1).at[at], pair_got.at[at], me.move(h=1), not0)
+    cross("a", top)
     text_partial(0, 0)
     chip_add(0, 0)
-
-    @pl.when(at0)
-    def _():
-        add(gp(0, 0), ring_got.at[1])
+    cross("b", bottom)
 
     @pl.when(is0 & (me.z < 2))
     def _():
@@ -518,7 +526,7 @@
 
     for name, at, j in (("p1b", bottom, 0), ("p2a", top, 1), ("p1a", top, 0), ("p2b", bottom, 1)):
         arrive(name, img_got.at[j, at])
-    img_out[...] = scale * (img_part[0] + img_got[0] + img_got[1])
+    img_out[...] = scale * (held(0, pl.ds(0, rows))[...] + img_got[0] + img_got[1])
     arrive_pieces("y", pair_got)
     txt_out[...] = scale * (txt_part[0] + ring_got[0] + pair_got[...])
 
@@ -562,7 +570,6 @@
             pltpu.VMEM((2 * N_TXT, rows), F32),
             pltpu.VMEM((3, 2 * N_IMG, rows), F32),
             pltpu.VMEM((len(DELTAS), 2 * N_TXT, rows), F32),
-            pltpu.VMEM((N_IMG, *block), F32),
             pltpu.VMEM((N_TXT, *block), F32),
             pltpu.VMEM((6, *block), F32),
             pltpu.VMEM((2, *block), F32),

time: 154 us -> 148 us (0.961)
  Pallas kernels: 148 us -> 142 us
    pallas_call x1, Pallas kernels: 148 us -> 142 us  [shards(): pl.pallas_call(functools.partial(kernel, rows), out_shape=(jax.ShapeDtype...]
where the time goes in v3:
time: 148 us
  Pallas kernels  142 us (96%)
  local copies, waits for them, and re-layouts  4.29 us (3%)
    pallas_call x1, Pallas kernels, shards(): pl.pallas_call(functools.partial(kernel, rows), out_shape=(jax.ShapeDtype...  142 us
    unnamed x4, local copies, waits for them, and re-layouts  3.02 us

profile of v3, /device:TPU:9, one launch (start us, length us, event | category | flops | bytes accessed | tf_op | source)
XLA Modules:
  0.0 147.9 jit_solution(14837828135860888511)
XLA Ops:
  1.3 142.3 %shard_map.66 = (f32[8,128]{1,0:T(8,128)}, f32[256,768]{1,0:T(8,128)}, f32[256,768]{1,0:T(8,128)}) custom-call(f32[1]{0:T(128)S(6)} %copy.9.scale_ref, f32[256,768]{1,0:T(8,128)} %img_ref.1, f32[256,768]{1,0:T(8,128)} %txt_ref.1), custom_call_target="tpu_custom_call" | custom-call | flops 28999999488 | bytes 4000000 | tf_op jit(solution)/shard_map/pallas_call | solution.py:547
  143.6 1.3 fusion
  144.9 0.0 copy-start
  144.9 2.1 %copy.10 = f32[256,768]{1,0:T(8,128)} copy(f32[256,768]{1,0:T(8,128)} %get-tuple-element.18) | data formatting | bytes 1572864
  147.0 0.0 copy-done
  147.0 0.9 copy.11
Async XLA Ops:
  144.9 2.1 %copy-start = (f32[256,768]{1,0:T(8,128)S(1)}, f32[256,768]{1,0:T(8,128)}, u32[]{:S(2)}) copy-start(f32[256,768]{1,0:T(8,128)} %get-tuple-element.19) | copy-start | bytes 2359300
